TPU v7x, 32 devices: a whole 2x2x4 slice. The times are simulated.
32 devices in a mesh: groups: 2 (over x), dp: 16 (over z, y, core).
Axes of the slice: x: 2, y: 2, z: 4, core: 2. Of those that a mesh axis runs over, the one named last changes fastest.
Arguments:
- tokens: bfloat16 [16384, 1024], P(('groups', 'dp')), parts along dimension 0, may hold values from -8 to 8
- lengths: int32 [32, 8], P(('groups', 'dp')), parts along dimension 0, may hold values from 1 to 256, 512 in all within a row
- input_weight: bfloat16 [1024, 3072], P(None, 'dp'), may hold values from -0.5 to 0.5
- output_weight: bfloat16 [1024, 1024], P(None, 'dp'), may hold values from -0.1875 to 0.1875
- norm_gain: float32 [1024], replicated, may hold values from 0.25 to 1.75
- expand_weight: bfloat16 [1024, 2048], P(None, 'dp'), may hold values from -0.1875 to 0.1875
- shrink_weight: bfloat16 [2048, 1024], P(None, 'dp'), may hold values from -0.125 to 0.125
- assigned: int32 [16384], P(('groups', 'dp')), parts along dimension 0, may hold values from 0 to 63, as said below
- owner_map: int32 [128], P('groups'), parts along dimension 0, may hold values from 0 to 63, each once
- centroids: bfloat16 [64, 1024], P('dp'), may hold values from -3 to 3
Outputs:
- filed: bfloat16 [128, 256, 1024], P(('groups', 'dp')), parts along dimension 0
There are 2 independent parts, one for each index of `groups`. A program takes and returns all parts, laid end to end along the dimension named above; an argument that names none is the same for every part. Nothing has to cross between parts.
Inputs may be any that keep to these rules, and one draw needn't show every extreme that they name: `assigned`: each device's 512 rows name no list more than 16 times, and one list is named exactly 16 times by the rows of every device. The 8 lengths of a device sum to 512; its passages lie end to end in its rows. `owner_map`: A permutation; the list with value p belongs to the device p // 4.
All inputs are finite; a program needn't handle non-finite values.
Results may differ from a plain program's by a relative error of at most 0.015.
Values may be sent and summed in bfloat16 or wider, within the bound.
No kernel may reach another device: no remote copies, remote signals or barrier semaphores. Data moves between devices by JAX's collectives and lax.ppermute only.
A program may use at most 128 MiB of HBM per device.

v0:
```python
import math

import jax
import jax.numpy as jnp
from jax import lax
from jax.sharding import PartitionSpec as P

HEADS = 16


norm_eps = 1e-06
ridge_term = 0.05


def layer_norm(values, gain_row):
    row_mean = jnp.mean(values, axis=-1, keepdims=True)
    centered = values - row_mean
    row_var = jnp.mean(centered * centered, axis=-1, keepdims=True)
    return centered * lax.rsqrt(row_var + norm_eps) * gain_row


def segment_ids(length_row, row_count):
    boundary = jnp.cumsum(length_row)
    position = jnp.arange(row_count, dtype=jnp.int32)
    return jnp.sum((position[:, None] >= boundary[None, :]).astype(jnp.int32), axis=1)


def attend(queries, keys_in, values_in, length_row, head_count):
    row_count, model_width = queries.shape
    head_dim = model_width // head_count
    segment = segment_ids(length_row, row_count)
    same_passage = segment[:, None] == segment[None, :]
    score_scale = 1.0 / math.sqrt(head_dim)

    def split_heads(matrix):
        return matrix.reshape(row_count, head_count, head_dim).transpose(1, 0, 2)

    def one_head(head_parts):
        query_head, key_head, value_head = head_parts
        scores = jnp.dot(query_head, key_head.T, preferred_element_type=jnp.float32) * score_scale
        scores = jnp.where(same_passage, scores, -1e30)
        weights = jax.nn.softmax(scores, axis=-1).astype(jnp.bfloat16)
        return jnp.dot(weights, value_head, preferred_element_type=jnp.float32).astype(jnp.bfloat16)

    mixed = lax.map(one_head, (split_heads(queries), split_heads(keys_in), split_heads(values_in)))
    return mixed.transpose(1, 0, 2).reshape(row_count, model_width)


def body(
    tokens,
    lengths,
    input_weight,
    output_weight,
    norm_gain,
    expand_weight,
    shrink_weight,
    assigned,
    owner_map,
    centroids,
):
    row_count, model_width = tokens.shape
    device_count = lax.axis_size("dp")
    projected = jnp.dot(
        tokens,
        lax.all_gather(input_weight, "dp", axis=1, tiled=True),
        preferred_element_type=jnp.float32,
    ).astype(jnp.bfloat16)
    attended = attend(
        projected[:, :model_width],
        projected[:, model_width : 2 * model_width],
        projected[:, 2 * model_width :],
        lengths[0],
        HEADS,
    )
    mixed_out = jnp.dot(
        attended,
        lax.all_gather(output_weight, "dp", axis=1, tiled=True),
        preferred_element_type=jnp.float32,
    )
    first_norm = layer_norm(tokens.astype(jnp.float32) + mixed_out, norm_gain).astype(jnp.bfloat16)
    product = jnp.dot(
        first_norm,
        lax.all_gather(expand_weight, "dp", axis=1, tiled=True),
        preferred_element_type=jnp.float32,
    )
    expanded = jax.nn.gelu(product, approximate=False).astype(jnp.bfloat16)
    reduced = jnp.dot(
        expanded,
        lax.all_gather(shrink_weight, "dp", axis=1, tiled=True),
        preferred_element_type=jnp.float32,
    )
    embedded = layer_norm(first_norm.astype(jnp.float32) + reduced, 1.0).astype(jnp.bfloat16)
    gram = lax.dot_general(
        embedded, embedded, (((0,), (0,)), ((), ())), preferred_element_type=jnp.float32
    )
    total_gram = lax.psum(gram, "dp")
    total_rows = row_count * device_count
    covariance = total_gram / total_rows + ridge_term * jnp.eye(model_width, dtype=jnp.float32)
    factor = jnp.linalg.cholesky(covariance)
    whitened = jax.scipy.linalg.solve_triangular(
        factor, embedded.astype(jnp.float32).T, lower=True
    ).T.astype(jnp.bfloat16)
    lists_owned = centroids.shape[0]
    list_total = lists_owned * device_count
    slot_count = max(2, 2 * row_count // list_total)
    choose = (assigned[:, None] == jnp.arange(list_total, dtype=jnp.int32)[None, :]).astype(
        jnp.int32
    )
    position = jnp.sum(choose * owner_map[None, :], axis=1)
    earlier = jnp.cumsum(choose, axis=0) - choose
    rank_in_list = jnp.sum(earlier * choose, axis=1)
    local_list = position % lists_owned
    target = position // lists_owned
    slot_index = (local_list * device_count + target) * slot_count + rank_in_list
    buffer_rows = lists_owned * device_count * slot_count
    layout = (lists_owned, device_count, slot_count)
    outgoing = jnp.zeros((buffer_rows, model_width), jnp.bfloat16).at[slot_index].set(whitened)
    marks = jnp.zeros((buffer_rows, 1), jnp.bfloat16).at[slot_index].set(1.0)
    incoming = lax.all_to_all(
        outgoing.reshape(layout + (model_width,)), "dp", split_axis=1, concat_axis=1, tiled=True
    )
    occupied = lax.all_to_all(
        marks.reshape(layout + (1,)), "dp", split_axis=1, concat_axis=1, tiled=True
    )
    difference = incoming.astype(jnp.float32) - centroids.astype(jnp.float32)[:, None, None, :]
    arrived = (difference * occupied.astype(jnp.float32)).astype(jnp.bfloat16)
    return arrived.reshape(lists_owned, device_count * slot_count, model_width)


def solution(mesh):
    in_specs = (
        P(("groups", "dp"), None),
        P(("groups", "dp"), None),
        P(None, "dp"),
        P(None, "dp"),
        P(),
        P(None, "dp"),
        P(None, "dp"),
        P(("groups", "dp")),
        P("groups"),
        P("dp", None),
    )
    out_specs = P(("groups", "dp"), None, None)
    return jax.shard_map(body, mesh=mesh, in_specs=in_specs, out_specs=out_specs, check_vma=False)
```

profile of v0, /device:TPU:13, one launch (start us, length us, event | category | flops | bytes accessed | tf_op | source)
XLA Modules:
  0.0 786.4 jit_solution(12079255056050850742)
XLA Ops:
  10.3 61.8 %all-gather.5.cloned.1.call-done = bf16[1024,3072]{0,1:T(8,128)(2,1)} async-done(((bf16[1024,192]{0,1:T(8,128)(2,1)}), bf16[1024,3072]{0,1:T(8,128)(2,1)}) %all-gather.5.cloned.1.call-update) | async-done | bytes 6291472 | tf_op jit(solution)/shard_map/all_gather | solution.py:65
  72.1 6.6 convolution_convert_fusion.1
  81.6 37.8 %while.13 = (s32[]{:T(128)}, bf16[16,512,64]{1,2,0:T(8,128)(2,1)}, bf16[16,512,64]{1,2,0:T(8,128)(2,1)S(1)}, bf16[16,512,64]{1,2,0:T(8,128)(2,1)S(1)}, bf16[16,5...) while((s32[]{:T(128)}, bf16[16,512,64]{1,2,0:T(8,128)(2,1)}, ...), condition=%wide.region_9.10_spmd.clone, body=%wide.region_6.9_spmd.clone.sunk | while | flops 69499904 | bytes 3424333 | solution.py:45
  119.4 3.3 fusion.136
  124.4 41.5 %all-gather.11.cloned.1.call-done = bf16[2048,1024]{0,1:T(8,128)(2,1)} async-done(((bf16[2048,64]{0,1:T(8,128)(2,1)}), bf16[2048,1024]{0,1:T(8,128)(2,1)}) %all-gather.11.cloned.1.call-update) | async-done | bytes 4194320 | tf_op jit(solution)/shard_map/all_gather | solution.py:89
  165.9 51.9 %all-gather.9.cloned.1.call-done = bf16[1024,2048]{1,0:T(8,128)(2,1)} async-done(((bf16[1024,128]{1,0:T(8,128)(2,1)}), bf16[1024,2048]{1,0:T(8,128)(2,1)}) %all-gather.9.cloned.1.call-update) | async-done | bytes 4194320 | tf_op jit(solution)/shard_map/all_gather | solution.py:83
  217.8 17.2 %fusion.137 = (f32[512]{0:T(512)S(1)}, f32[512,1024]{1,0:T(8,128)S(1)}) fusion(bf16[2048,1024]{0,1:T(8,128)(2,1)} %all-gather.11.cloned.1.call-done, bf16[1024,2048]{1,0:T(8,128)(2,1)} %all-gather.9.cloned.1.call-done, f32[512,1024]{1,0:T(8,128)} %copy-done.3, f32[1024]{0:T(1024)S(1)} %copy-done.9, f32[512]{0:T(512)S(1)} %add_rsqrt_fusion.1, ...), kind=kOutput, calls=%fused_computation.271 | convolution fusion | flops 4368891392 | bytes 12593152 | tf_op jit(solution)/shard_map/dot_general | solution.py:87
  237.0 3.3 fusion.138
  242.0 3.8 scatter_custom_fusion.1
  246.5 6.4 all-to-all-start.1
  252.9 98.4 %all-reduce.3.cloned.1.call-done = f32[1024,1024]{0,1:T(8,128)} async-done(((f32[1024,1024]{0,1:T(8,128)}), f32[1024,1024]{0,1:T(8,128)}) %all-reduce.3.cloned.1.call-update) | async-done | bytes 4194320 | tf_op jit(solution)/shard_map/psum | solution.py:96
  351.3 5.0 select_add_fusion
  356.4 5.5 copy.138
  361.9 4.5 fusion.19
  368.3 11.7 %cholesky.222 = f32[128,128]{1,0:T(8,128)S(1)} custom-call(f32[128,128]{1,0:T(8,128)S(1)} %cholesky.577), custom_call_target="Cholesky" | custom-call | tf_op jit(solution)/shard_map/jit(cholesky)/cholesky | solution.py:99
  380.0 9.8 %custom-call.63 = f32[1,128,128]{1,2,0:T(8,128)S(1)} custom-call(f32[1,128,128]{2,1,0:T(8,128)S(1)} %get-tuple-element.166), custom_call_target="InvertDiagBlocksLowerTriangular" | custom-call | tf_op jit(solution)/shard_map/jit(cholesky)/cholesky | solution.py:99
  393.0 11.7 %cholesky.243 = f32[128,128]{1,0:T(8,128)S(1)} custom-call(f32[128,128]{1,0:T(8,128)S(1)} %cholesky.581), custom_call_target="Cholesky" | custom-call | tf_op jit(solution)/shard_map/jit(cholesky)/cholesky | solution.py:99
  405.3 9.8 %custom-call.64 = f32[1,128,128]{1,2,0:T(8,128)S(1)} custom-call(f32[1,128,128]{2,1,0:T(8,128)S(1)} %get-tuple-element.164), custom_call_target="InvertDiagBlocksLowerTriangular" | custom-call | tf_op jit(solution)/shard_map/jit(cholesky)/cholesky | solution.py:99
  418.2 2.4 convolution_subtract_fusion.1
  420.6 11.7 %cholesky.466 = f32[128,128]{1,0:T(8,128)S(1)} custom-call(f32[128,128]{1,0:T(8,128)S(1)} %cholesky.586), custom_call_target="Cholesky" | custom-call | tf_op jit(solution)/shard_map/jit(cholesky)/cholesky | solution.py:99
  433.1 9.8 %custom-call.65 = f32[1,128,128]{1,2,0:T(8,128)S(1)} custom-call(f32[1,128,128]{2,1,0:T(8,128)S(1)} %get-tuple-element.162), custom_call_target="InvertDiagBlocksLowerTriangular" | custom-call | tf_op jit(solution)/shard_map/jit(cholesky)/cholesky | solution.py:99
  444.2 3.5 convolution_subtract_fusion.2
  447.7 11.7 %cholesky.485 = f32[128,128]{1,0:T(8,128)S(1)} custom-call(f32[128,128]{1,0:T(8,128)S(1)} %cholesky.591), custom_call_target="Cholesky" | custom-call | tf_op jit(solution)/shard_map/jit(cholesky)/cholesky | solution.py:99
  460.2 9.8 %custom-call.66 = f32[1,128,128]{1,2,0:T(8,128)S(1)} custom-call(f32[1,128,128]{2,1,0:T(8,128)S(1)} %get-tuple-element.160), custom_call_target="InvertDiagBlocksLowerTriangular" | custom-call | tf_op jit(solution)/shard_map/jit(cholesky)/cholesky | solution.py:99
  471.2 3.1 convolution_subtract_fusion.10
  474.4 11.9 %cholesky.504 = f32[128,128]{1,0:T(8,128)S(1)} custom-call(f32[128,128]{1,0:T(8,128)S(1)} %cholesky.596), custom_call_target="Cholesky" | custom-call | tf_op jit(solution)/shard_map/jit(cholesky)/cholesky | solution.py:99
  487.0 9.8 %custom-call.67 = f32[1,128,128]{1,2,0:T(8,128)S(1)} custom-call(f32[1,128,128]{2,1,0:T(8,128)S(1)} %get-tuple-element.158), custom_call_target="InvertDiagBlocksLowerTriangular" | custom-call | tf_op jit(solution)/shard_map/jit(cholesky)/cholesky | solution.py:99
  497.9 3.1 convolution_subtract_fusion.11
  501.0 11.7 %cholesky.524 = f32[128,128]{1,0:T(8,128)S(1)} custom-call(f32[128,128]{1,0:T(8,128)S(1)} %cholesky.601), custom_call_target="Cholesky" | custom-call | tf_op jit(solution)/shard_map/jit(cholesky)/cholesky | solution.py:99
  513.5 9.8 %custom-call.68 = f32[1,128,128]{1,2,0:T(8,128)S(1)} custom-call(f32[1,128,128]{2,1,0:T(8,128)S(1)} %get-tuple-element.156), custom_call_target="InvertDiagBlocksLowerTriangular" | custom-call | tf_op jit(solution)/shard_map/jit(cholesky)/cholesky | solution.py:99
  524.3 3.1 convolution_subtract_fusion.12
  527.4 11.7 %cholesky.544 = f32[128,128]{1,0:T(8,128)S(1)} custom-call(f32[128,128]{1,0:T(8,128)S(1)} %cholesky.606), custom_call_target="Cholesky" | custom-call | tf_op jit(solution)/shard_map/jit(cholesky)/cholesky | solution.py:99
  539.9 9.8 %custom-call.69 = f32[1,128,128]{1,2,0:T(8,128)S(1)} custom-call(f32[1,128,128]{2,1,0:T(8,128)S(1)} %get-tuple-element.154), custom_call_target="InvertDiagBlocksLowerTriangular" | custom-call | tf_op jit(solution)/shard_map/jit(cholesky)/cholesky | solution.py:99
  552.7 11.7 %cholesky.562 = f32[128,128]{1,0:T(8,128)S(1)} custom-call(f32[128,128]{1,0:T(8,128)S(1)} %convolution_subtract_fusion.13), custom_call_target="Cholesky" | custom-call | tf_op jit(solution)/shard_map/jit(cholesky)/cholesky | solution.py:99
  575.0 5.0 select_select_fusion
  579.9 28.0 %while.12 = (s32[]{:T(128)}, f32[1024,1024]{0,1:T(8,128)}, s32[8,2]{0,1:T(2,128)S(1)}, f32[8,128,128]{2,1,0:T(8,128)}, s32[]{:T(128)}) while((s32[]{:T(128)}, f32[1024,1024]{0,1:T(8,128)}, s32[8,2]{0,1:T(2,128)S(1)}, f32[8,128,128]{2,1,0:T(8,128)}, s32[]{:T(128)}) %tuple.82), condition=%wide.while_cond, body=%wide.while_body.sunk | while | flops 2 | bytes 393829 | solution.py:100
  580.5 2.2 dynamic-slice.7
  584.1 2.2 dynamic-slice.7
  587.6 2.2 dynamic-slice.7
  608.0 80.2 %custom-call.70 = f32[8,128,128]{1,2,0:T(8,128)} custom-call(f32[8,128,128]{2,1,0:T(8,128)} %get-tuple-element.45), custom_call_target="InvertDiagBlocksLowerTriangular" | custom-call | tf_op jit(solution)/shard_map/jit(_solve_triangular)/triangular_solve | solution.py:100
  696.5 2.4 convolution_subtract_fusion.8
  699.9 2.8 convolution_subtract_fusion.9
  704.1 3.2 convolution_subtract_fusion.4
  708.5 3.6 convolution_subtract_fusion.7
  713.2 4.3 convolution_subtract_fusion.3
  720.1 3.2 scatter_custom_fusion
  724.9 5.5 all-to-all-start
  730.4 47.4 %all-to-all-done = bf16[4,16,16,1024]{3,2,0,1:T(8,128)(2,1)S(1)} async-done(((bf16[4,16,16,1024]{3,2,0,1:T(8,128)(2,1)}), bf16[4,16,16,1024]{3,2,0,1:T(8,128)(2,1)S(1)}, u32[]{:S(2)}, u32[]{:S(2)}) %all-to-all-start) | async-done | bytes 2097184 | tf_op jit(solution)/shard_map/all_to_all | solution.py:119
  (216 shorter events, 116.1 us)
Async XLA Ops:
  6.5 65.6 %all-gather.5.cloned.1.call-start = ((), (), s32[]{:S(2)}) async-start(), calls=%async_computation.2 | async-start | bytes 6684672 | tf_op jit(solution)/shard_map/all_gather | solution.py:65
  7.3 112.2 %all-gather.7.cloned.1.call-start = ((), (), s32[]{:S(2)}) async-start(), calls=%async_computation.3 | async-start | bytes 2228224 | tf_op jit(solution)/shard_map/all_gather | solution.py:77
  8.0 157.9 %all-gather.11.cloned.1.call-start = ((), (), s32[]{:S(2)}) async-start(), calls=%async_computation.5 | async-start | bytes 4456448 | tf_op jit(solution)/shard_map/all_gather | solution.py:89
  8.7 209.1 %all-gather.9.cloned.1.call-start = ((), (), s32[]{:S(2)}) async-start(), calls=%async_computation.4 | async-start | bytes 4456448 | tf_op jit(solution)/shard_map/all_gather | solution.py:83
  9.3 342.0 %all-reduce.3.cloned.1.call-start = ((), (), s32[]{:S(2)}) async-start(), calls=%async_computation.6 | async-start | bytes 8388608 | tf_op jit(solution)/shard_map/psum | solution.py:96
  81.5 37.9 %copy-start.8 = (bf16[512,1024]{1,0:T(8,128)(2,1)S(1)}, bf16[512,1024]{1,0:T(8,128)(2,1)}, u32[]{:S(2)}) copy-start(bf16[512,1024]{1,0:T(8,128)(2,1)} %param.12) | copy-start | bytes 3145732
  119.4 98.4 %copy-start.9 = (f32[1024]{0:T(1024)S(1)}, f32[1024]{0:T(1024)}, u32[]{:S(2)}) copy-start(f32[1024]{0:T(1024)} %param.16) | copy-start | bytes 12292
  122.7 1.3 copy-start.3
  237.0 3.3 copy-start.5
  240.3 1.5 copy-start.7
  246.5 478.4 %all-to-all-start.1 = ((bf16[4,16,16,1]{2,0,3,1:T(4,128)(2,1)}), bf16[4,16,16,1]{2,0,3,1:T(4,128)(2,1)S(1)}, u32[]{:S(2)}, u32[]{:S(2)}) async-start(bf16[4,16,16,1]{2,0,3,1:T(4,128)(2,1)} %copy.165), calls=%async_computation.1 | async-start | bytes 32768 | tf_op jit(solution)/shard_map/all_to_all | solution.py:122
  366.3 1.9 copy-start.1
  416.2 2.0 copy-start
  575.0 115.2 %copy-start.2 = (f32[1024,512]{0,1:T(8,128)S(1)}, f32[1024,512]{0,1:T(8,128)}, u32[]{:S(2)}) copy-start(f32[1024,512]{0,1:T(8,128)} %get-tuple-element.127) | copy-start | bytes 6291460
  688.2 7.2 copy-start.4
  723.4 7.0 copy-start.6
  724.9 52.9 %all-to-all-start = ((bf16[4,16,16,1024]{3,2,0,1:T(8,128)(2,1)}), bf16[4,16,16,1024]{3,2,0,1:T(8,128)(2,1)S(1)}, u32[]{:S(2)}, u32[]{:S(2)}) async-start(bf16[4,16,16,1024]{3,2,0,1:T(8,128)(2,1)} %copy.163), calls=%async_computation | async-start | bytes 4194304 | tf_op jit(solution)/shard_map/all_to_all | solution.py:119
Sparse Core Ops, SparseCore 0:
  9.6 62.4 all-gather.4
  74.3 39.0 all-gather.6
  115.5 50.2 all-gather.10
  167.9 49.8 all-gather.8
  240.4 110.8 all-reduce.2
where the time goes:
time: 793 us; the launch traced here: 786 us
  waiting for transfers between devices  304 us (38%)
  other arithmetic  272 us (34%)
  matrix products  121 us (15%)
  local copies, waits for them, and re-layouts  58.5 us (7%)
  between operations  19 us (2%)
  starting transfers between devices  12.1 us (2%)
    another operation x30, other arithmetic, body(): factor = jnp.linalg.cholesky(covariance)  168 us
    psum x1, waiting for transfers between devices, body(): total_gram = lax.psum(gram, 'dp')  98.4 us
    another operation x3, other arithmetic, body(): jax.scipy.linalg.solve_triangular(factor, embedded.astype(jnp.float32).T,...  85.2 us
    all_gather x1, waiting for transfers between devices, body(): lax.all_gather(input_weight, 'dp', axis=1, tiled=True)  61.8 us
    all_gather x1, waiting for transfers between devices, body(): lax.all_gather(expand_weight, 'dp', axis=1, tiled=True)  51.9 us
    all_to_all x1, waiting for transfers between devices, body(): lax.all_to_all(outgoing.reshape(layout + (model_width,)), 'dp', split_axi...  47.4 us
    all_gather x1, waiting for transfers between devices, body(): lax.all_gather(shrink_weight, 'dp', axis=1, tiled=True)  41.5 us
    another operation x15, matrix products, body(): jax.scipy.linalg.solve_triangular(factor, embedded.astype(jnp.float32).T,...  29.9 us
  transfers between devices with their start and end apart: 7, of which 5 were waited for; matrix products, arithmetic and copies ran while one was open for 54% of the time, Pallas kernels for 0%

commit v1 on v0

--- a/solution.py
+++ b/solution.py
@@ -1,8 +1,11 @@
+import functools
 import math
 
 import jax
 import jax.numpy as jnp
 from jax import lax
+from jax.experimental import pallas as pl
+from jax.experimental.pallas import tpu as pltpu
 from jax.sharding import PartitionSpec as P
 
 HEADS = 16
@@ -44,6 +47,144 @@
 
     mixed = lax.map(one_head, (split_heads(queries), split_heads(keys_in), split_heads(values_in)))
     return mixed.transpose(1, 0, 2).reshape(row_count, model_width)
+
+
+BLOCK = 128
+PANEL = 8
+
+
+def split_bf16(value):
+    high = value.astype(jnp.bfloat16)
+    return high, (value - high.astype(jnp.float32)).astype(jnp.bfloat16)
+
+
+def dot3(left, right, dims):
+    lh, ll = left
+    rh, rl = right
+    dot = functools.partial(lax.dot_general, dimension_numbers=(dims, ((), ())), preferred_element_type=jnp.float32)
+    return dot(lh, rh) + (dot(lh, rl) + dot(ll, rh))
+
+
+def diagonal_inverse(rows):
+    count = len(rows)
+    lane = lax.broadcasted_iota(jnp.int32, (PANEL, BLOCK), 1)
+    sub = lax.broadcasted_iota(jnp.int32, (PANEL, BLOCK), 0)
+    shape = (PANEL, BLOCK)
+    rows = list(rows)
+    result = []
+    for p in range(count):
+        first = PANEL * p
+        panel = rows[p]
+        inside = (lane >= first) & (lane < first + PANEL)
+        spread = [jnp.broadcast_to(panel[:, first + t : first + t + 1], shape) for t in range(PANEL)]
+        entry = [[jnp.broadcast_to(spread[b][a : a + 1, :], shape) for b in range(a + 1)] for a in range(PANEL)]
+        columns = [
+            [jnp.broadcast_to(rows[i][:, first + t : first + t + 1], shape) for t in range(PANEL)]
+            for i in range(p + 1, count)
+        ]
+        forward = [
+            jnp.where(inside, jnp.where(lane == first + t, 1.0, 0.0), jnp.broadcast_to(panel[t : t + 1, :], shape))
+            for t in range(PANEL)
+        ]
+        ratio = [[None] * PANEL for _ in range(PANEL)]
+        kept = jnp.zeros(shape, jnp.float32)
+        solved = [None] * PANEL
+        for t in range(PANEL):
+            root = lax.rsqrt(entry[t][t])
+            inverse = root * root
+            for a in range(t + 1, PANEL):
+                ratio[a][t] = entry[a][t] * inverse
+            for a in range(t + 1, PANEL):
+                for b in range(t + 1, a + 1):
+                    entry[a][b] = entry[a][b] - ratio[a][t] * entry[b][t]
+            kept = jnp.where(sub == t, forward[t] * root, kept)
+            solved[t] = forward[t] * inverse
+            for a in range(t + 1, PANEL):
+                forward[a] = forward[a] - ratio[a][t] * forward[t]
+        for t in range(PANEL - 1, 0, -1):
+            for a in range(t):
+                solved[a] = solved[a] - ratio[t][a] * solved[t]
+        result.append(jnp.where(lane <= first + sub, kept, 0.0))
+        for i in range(p + 1, count):
+            col = columns[i - p - 1]
+            terms = [col[t] * solved[t] for t in range(PANEL)]
+            while len(terms) > 1:
+                terms = [a + b for a, b in zip(terms[::2], terms[1::2])]
+            rows[i] = jnp.where(inside, 0.0, rows[i]) - terms[0]
+    return result
+
+
+def factor_kernel(scale, ridge, gram_ref, out_ref, work):
+    width = gram_ref.shape[0]
+    blocks = width // BLOCK
+    eye = (
+        lax.broadcasted_iota(jnp.int32, (BLOCK, BLOCK), 0) == lax.broadcasted_iota(jnp.int32, (BLOCK, BLOCK), 1)
+    ).astype(jnp.float32)
+
+    def load(i, carry):
+        at = pl.ds(pl.multiple_of(i * BLOCK, BLOCK), BLOCK)
+        work[at, :] = gram_ref[at, :] * scale
+        work[at, at] = work[at, at] + ridge * eye
+        return carry
+
+    lax.fori_loop(0, blocks, load, 0)
+
+    def step(j, carry):
+        at = pl.ds(pl.multiple_of(j * BLOCK, BLOCK), BLOCK)
+        diagonal = work[at, at]
+        inverse = jnp.concatenate(
+            diagonal_inverse([diagonal[PANEL * i : PANEL * (i + 1), :] for i in range(BLOCK // PANEL)]), axis=0
+        )
+        pair = split_bf16(inverse)
+        work[at, at] = eye
+        scaled = dot3(pair, split_bf16(work[at, :]), ((1,), (0,)))
+        work[at, :] = scaled
+        scaled_pair = split_bf16(scaled)
+
+        def update(i, carry):
+            here = pl.ds(pl.multiple_of(i * BLOCK, BLOCK), BLOCK)
+            left = dot3(split_bf16(work[here, at]), pair, ((1,), (1,)))
+            work[here, at] = jnp.zeros((BLOCK, BLOCK), jnp.float32)
+            work[here, :] = work[here, :] - dot3(split_bf16(left), scaled_pair, ((1,), (0,)))
+            return carry
+
+        lax.fori_loop(j + 1, blocks, update, 0)
+        column = lax.broadcasted_iota(jnp.int32, (BLOCK, width), 1)
+        out_ref[at, :] = jnp.where(column < (j + 1) * BLOCK, scaled, 0.0).astype(out_ref.dtype)
+        return carry
+
+    lax.fori_loop(0, blocks, step, 0)
+
+
+def inverse_factor(gram, scale, ridge):
+    width = gram.shape[0]
+    return pl.pallas_call(
+        functools.partial(factor_kernel, scale, ridge),
+        out_shape=jax.ShapeDtypeStruct((width, width), jnp.bfloat16),
+        in_specs=[pl.BlockSpec(memory_space=pltpu.VMEM)],
+        out_specs=pl.BlockSpec(memory_space=pltpu.VMEM),
+        scratch_shapes=[pltpu.VMEM((width, width), jnp.float32)],
+        compiler_params=pltpu.CompilerParams(vmem_limit_bytes=40 * 1024 * 1024),
+    )(gram)
+
+
+EMPTY = 64.0
+
+
+def slots_of(assigned, owner_map, lists_owned, slot_count):
+    row_count = assigned.shape[0]
+    choose = assigned[:, None] == jnp.arange(owner_map.shape[0], dtype=jnp.int32)[None, :]
+    position = jnp.sum(jnp.where(choose, owner_map[None, :], 0), axis=1)
+    order = jnp.arange(row_count, dtype=jnp.int32)
+    earlier = (assigned[:, None] == assigned[None, :]) & (order[:, None] > order[None, :])
+    rank = jnp.sum(earlier.astype(jnp.int32), axis=1)
+    return position * slot_count + rank
+
+
+def place_rows(rows, slot_index, slot_total):
+    chosen = jnp.arange(slot_total, dtype=jnp.int32)[:, None] == slot_index[None, :]
+    placed = jnp.dot(chosen.astype(jnp.bfloat16), rows, preferred_element_type=jnp.float32)
+    return jnp.where(jnp.any(chosen, axis=1, keepdims=True), placed, EMPTY).astype(jnp.bfloat16)
 
 
 def body(
@@ -90,41 +231,30 @@
         preferred_element_type=jnp.float32,
     )
     embedded = layer_norm(first_norm.astype(jnp.float32) + reduced, 1.0).astype(jnp.bfloat16)
-    gram = lax.dot_general(
-        embedded, embedded, (((0,), (0,)), ((), ())), preferred_element_type=jnp.float32
-    )
-    total_gram = lax.psum(gram, "dp")
-    total_rows = row_count * device_count
-    covariance = total_gram / total_rows + ridge_term * jnp.eye(model_width, dtype=jnp.float32)
-    factor = jnp.linalg.cholesky(covariance)
-    whitened = jax.scipy.linalg.solve_triangular(
-        factor, embedded.astype(jnp.float32).T, lower=True
-    ).T.astype(jnp.bfloat16)
     lists_owned = centroids.shape[0]
     list_total = lists_owned * device_count
     slot_count = max(2, 2 * row_count // list_total)
-    choose = (assigned[:, None] == jnp.arange(list_total, dtype=jnp.int32)[None, :]).astype(
-        jnp.int32
-    )
-    position = jnp.sum(choose * owner_map[None, :], axis=1)
-    earlier = jnp.cumsum(choose, axis=0) - choose
-    rank_in_list = jnp.sum(earlier * choose, axis=1)
-    local_list = position % lists_owned
-    target = position // lists_owned
-    slot_index = (local_list * device_count + target) * slot_count + rank_in_list
-    buffer_rows = lists_owned * device_count * slot_count
-    layout = (lists_owned, device_count, slot_count)
-    outgoing = jnp.zeros((buffer_rows, model_width), jnp.bfloat16).at[slot_index].set(whitened)
-    marks = jnp.zeros((buffer_rows, 1), jnp.bfloat16).at[slot_index].set(1.0)
+    slot_index = slots_of(assigned, owner_map, lists_owned, slot_count)
+    outgoing = place_rows(embedded, slot_index, list_total * slot_count)
     incoming = lax.all_to_all(
-        outgoing.reshape(layout + (model_width,)), "dp", split_axis=1, concat_axis=1, tiled=True
-    )
-    occupied = lax.all_to_all(
-        marks.reshape(layout + (1,)), "dp", split_axis=1, concat_axis=1, tiled=True
-    )
-    difference = incoming.astype(jnp.float32) - centroids.astype(jnp.float32)[:, None, None, :]
-    arrived = (difference * occupied.astype(jnp.float32)).astype(jnp.bfloat16)
-    return arrived.reshape(lists_owned, device_count * slot_count, model_width)
+        outgoing.reshape(device_count, lists_owned, slot_count, model_width),
+        "dp",
+        split_axis=0,
+        concat_axis=0,
+        tiled=True,
+    )
+    gram = lax.dot_general(
+        embedded, embedded, (((0,), (0,)), ((), ())), preferred_element_type=jnp.float32
+    )
+    total_gram = lax.psum(gram, "dp")
+    inverse = inverse_factor(total_gram, 1.0 / (row_count * device_count), ridge_term)
+    arrived = incoming.transpose(1, 0, 2, 3).reshape(-1, model_width)
+    whitened = lax.dot_general(
+        arrived, inverse, (((1,), (1,)), ((), ())), preferred_element_type=jnp.float32
+    ).reshape(lists_owned, device_count * slot_count, model_width)
+    occupied = arrived[:, :1].reshape(lists_owned, device_count * slot_count, 1) < EMPTY
+    residual = whitened - centroids.astype(jnp.float32)[:, None, :]
+    return jnp.where(occupied, residual, 0.0).astype(jnp.bfloat16)
 
 
 def solution(mesh):

time: 793 us -> 481 us (0.61)
  other arithmetic: 272 us -> 7.1 us
  Pallas kernels: 0 us -> 66.2 us
  local copies, waits for them, and re-layouts: 58.5 us -> 9.35 us
  matrix products: 121 us -> 73 us
    another operation x36 -> x1, other arithmetic: 255 us -> 0.83 us  [the longest x30 168 us: body(): factor = jnp.linalg.cholesky(covariance)]
    pallas_call x0 -> x1, Pallas kernels: none -> 66.2 us  [inverse_factor(): pl.pallas_call(functools.partial(factor_kernel, scale, ridge), out_shape=...]
    another operation x29 -> x0, matrix products: 56.2 us -> none  [the longest x15 29.9 us: body(): jax.scipy.linalg.solve_triangular(factor, embedded.astype(jnp.float32).T,...]
    all_to_all x2 -> x1, waiting for transfers between devices: 47.4 us -> 0.01 us  [body(): lax.all_to_all(outgoing.reshape(device_count, lists_owned, slot_count, mo...]
    psum x1, waiting for transfers between devices: 98.4 us -> 145 us  [body(): total_gram = lax.psum(gram, 'dp')]
    another operation x69 -> x0, local copies, waits for them, and re-layouts: 33.8 us -> none
    dot_general x16, matrix products: 5.85 us -> 19.4 us  [one_head(): jnp.dot(query_head, key_head.T, preferred_element_type=jnp.float32)]
    dot_general x16, matrix products: 28.6 us -> 15.2 us  [one_head(): jnp.dot(weights, value_head, preferred_element_type=jnp.float32)]
  transfers between devices with their start and end apart: 7 -> 6, of which waited for: 5 -> 4; matrix products, arithmetic and copies ran while one was open for 54% -> 12% of each run, Pallas kernels for 0% -> 14%
where the time goes in v1:
time: 481 us; the launch traced here: 477 us
  waiting for transfers between devices  301 us (63%)
  matrix products  73 us (15%)
  Pallas kernels  66.2 us (14%)
  between operations  13.3 us (3%)
  local copies, waits for them, and re-layouts  9.35 us (2%)
  starting transfers between devices  7.5 us (2%)
  other arithmetic  7.1 us (1%)
    psum x1, waiting for transfers between devices, body(): total_gram = lax.psum(gram, 'dp')  145 us
    pallas_call x1, Pallas kernels, inverse_factor(): pl.pallas_call(functools.partial(factor_kernel, scale, ridge), out_shape=...  66.2 us
    all_gather x1, waiting for transfers between devices, body(): lax.all_gather(input_weight, 'dp', axis=1, tiled=True)  59.8 us
    all_gather x1, waiting for transfers between devices, body(): lax.all_gather(expand_weight, 'dp', axis=1, tiled=True)  51.9 us
    all_gather x1, waiting for transfers between devices, body(): lax.all_gather(shrink_weight, 'dp', axis=1, tiled=True)  41.5 us
    dot_general x16, matrix products, one_head(): jnp.dot(query_head, key_head.T, preferred_element_type=jnp.float32)  19.4 us
    dot_general x1, matrix products, body(): jnp.dot(expanded, lax.all_gather(shrink_weight, 'dp', axis=1, tiled=True)...  17 us
    dot_general x16, matrix products, one_head(): jnp.dot(weights, value_head, preferred_element_type=jnp.float32)  15.2 us
  transfers between devices with their start and end apart: 6, of which 4 were waited for; matrix products, arithmetic and copies ran while one was open for 12% of the time, Pallas kernels for 14%

profile of v1, /device:TPU:13, one launch (start us, length us, event | category | flops | bytes accessed | tf_op | source)
XLA Modules:
  0.0 477.5 jit_solution(2568736986907818469)
XLA Ops:
  10.2 1.0 convert_reduce_fusion
  12.3 59.8 %all-gather.5.cloned.1.call-done = bf16[1024,3072]{0,1:T(8,128)(2,1)} async-done(((bf16[1024,192]{0,1:T(8,128)(2,1)}), bf16[1024,3072]{0,1:T(8,128)(2,1)}) %all-gather.5.cloned.1.call-update) | async-done | bytes 6291472 | tf_op jit(solution)/shard_map/all_gather | solution.py:206
  72.1 6.6 %convolution_convert_fusion.1 = bf16[512,3072]{1,0:T(8,128)(2,1)S(1)} fusion(bf16[512,1024]{1,0:T(8,128)(2,1)} %param.12, bf16[1024,3072]{0,1:T(8,128)(2,1)} %all-gather.5.cloned.1.call-done), kind=kOutput, calls=%fused_computation.20 | convolution fusion | flops 3222798336 | bytes 10485760 | tf_op jit(solution)/shard_map/dot_general | solution.py:204
  79.0 1.3 copy.36
  81.5 37.8 %while.11 = (s32[]{:T(128)}, bf16[16,512,64]{1,2,0:T(8,128)(2,1)}, bf16[16,512,64]{1,2,0:T(8,128)(2,1)}, bf16[16,512,64]{1,2,0:T(8,128)(2,1)S(1)}, bf16[16,512,6...) while((s32[]{:T(128)}, bf16[16,512,64]{1,2,0:T(8,128)(2,1)}, ...), condition=%wide.region_8.9_spmd.clone, body=%wide.region_5.8_spmd.clone.sunk | while | flops 69499904 | bytes 3424333 | solution.py:48
  81.5 1.3 fusion.85
  83.0 0.9 fusion.87
  83.9 1.2 fusion.85
  85.3 0.9 fusion.87
  86.3 1.2 fusion.85
  87.7 0.9 fusion.87
  88.6 1.2 fusion.85
  91.0 1.2 fusion.85
  92.4 0.9 fusion.87
  93.4 1.2 fusion.85
  94.8 0.9 fusion.87
  95.7 1.2 fusion.85
  97.1 0.9 fusion.87
  98.1 1.2 fusion.85
  99.5 0.9 fusion.87
  100.4 1.2 fusion.85
  101.8 0.9 fusion.87
  102.8 1.2 fusion.85
  104.2 0.9 fusion.87
  105.1 1.2 fusion.85
  106.5 0.9 fusion.87
  107.5 1.2 fusion.85
  108.9 0.9 fusion.87
  109.8 1.2 fusion.85
  111.2 0.9 fusion.87
  112.2 1.2 fusion.85
  114.5 1.2 fusion.85
  116.0 0.9 fusion.87
  116.9 1.2 fusion.85
  119.3 3.3 fusion.71
  122.6 1.3 copy-done.2
  124.3 41.5 %all-gather.11.cloned.1.call-done = bf16[2048,1024]{0,1:T(8,128)(2,1)} async-done(((bf16[2048,64]{0,1:T(8,128)(2,1)}), bf16[2048,1024]{0,1:T(8,128)(2,1)}) %all-gather.11.cloned.1.call-update) | async-done | bytes 4194320 | tf_op jit(solution)/shard_map/all_gather | solution.py:230
  165.8 51.9 %all-gather.9.cloned.1.call-done = bf16[1024,2048]{1,0:T(8,128)(2,1)} async-done(((bf16[1024,128]{1,0:T(8,128)(2,1)}), bf16[1024,2048]{1,0:T(8,128)(2,1)}) %all-gather.9.cloned.1.call-update) | async-done | bytes 4194320 | tf_op jit(solution)/shard_map/all_gather | solution.py:224
  217.8 17.0 %fusion.72 = (f32[512]{0:T(512)S(1)}, f32[512,1024]{1,0:T(8,128)S(1)}) fusion(bf16[2048,1024]{0,1:T(8,128)(2,1)} %all-gather.11.cloned.1.call-done, bf16[1024,2048]{1,0:T(8,128)(2,1)} %all-gather.9.cloned.1.call-done, f32[512,1024]{1,0:T(8,128)} %copy-done.2, f32[1024]{0:T(1024)S(1)} %copy-done.5, f32[512]{0:T(512)S(1)} %add_rsqrt_fusion.1, ...), kind=kOutput, calls=%fused_computation.101 | convolution fusion | flops 4368891392 | bytes 12593152 | tf_op jit(solution)/shard_map/dot_general | solution.py:228
  235.1 2.7 select_convert_fusion.1
  237.9 7.3 %all-to-all-start = ((bf16[16,4,16,1024]{3,2,1,0:T(8,128)(2,1)}), bf16[16,4,16,1024]{3,2,1,0:T(8,128)(2,1)}, u32[]{:S(2)}, u32[]{:S(2)}) async-start(bf16[16,4,16,1024]{3,2,1,0:T(8,128)(2,1)} %bitcast.10), calls=%async_computation | async-start | bytes 4194304 | tf_op jit(solution)/shard_map/all_to_all | solution.py:239
  245.3 3.6 fusion.67
  248.9 145.0 %all-reduce.2.cloned.1.call-done.gram_ref = f32[1024,1024]{1,0:T(8,128)} async-done(((f32[1024,1024]{1,0:T(8,128)}), f32[1024,1024]{1,0:T(8,128)}) %all-reduce.2.cloned.1.call-update) | async-done | bytes 4194320 | tf_op jit(solution)/shard_map/psum | solution.py:249
  393.9 2.2 copy-done
  396.1 66.2 %shard_map.100 = bf16[1024,1024]{1,0:T(8,128)(2,1)S(1)} custom-call(f32[1024,1024]{1,0:T(8,128)S(1)} %copy-done), custom_call_target="tpu_custom_call" | custom-call | tf_op jit(solution)/shard_map/pallas_call | solution.py:161
  462.3 1.8 copy.42
  464.1 1.3 copy-done.1
  465.7 5.3 %select_convert_fusion = bf16[4,256,1024]{2,1,0:T(8,128)(2,1)} fusion(f32[4,1024]{1,0:T(4,128)S(1)} %convert_element_type.49, pred[4,256]{1,0:T(4,128)(4,1)S(1)} %lt.19, bf16[4,256,1024]{2,1,0:T(8,128)(2,1)} %bitcast.61, bf16[1024,1024]{1,0:T(8,128)(2,1)S(1)} %shard_map.100), kind=kOutput, calls=%fused_computation.24 | convolution fusion | flops 2150629376 | bytes 6308864 | tf_op jit(solution)/shard_map/dot_general | solution.py:252
  (58 shorter events, 13.1 us)
Async XLA Ops:
  6.5 65.6 %all-gather.5.cloned.1.call-start = ((), (), s32[]{:S(2)}) async-start(), calls=%async_computation.1 | async-start | bytes 6684672 | tf_op jit(solution)/shard_map/all_gather | solution.py:206
  7.3 112.0 %all-gather.7.cloned.1.call-start = ((), (), s32[]{:S(2)}) async-start(), calls=%async_computation.2 | async-start | bytes 2228224 | tf_op jit(solution)/shard_map/all_gather | solution.py:218
  8.0 157.8 %all-gather.11.cloned.1.call-start = ((), (), s32[]{:S(2)}) async-start(), calls=%async_computation.4 | async-start | bytes 4456448 | tf_op jit(solution)/shard_map/all_gather | solution.py:230
  8.7 209.0 %all-gather.9.cloned.1.call-start = ((), (), s32[]{:S(2)}) async-start(), calls=%async_computation.3 | async-start | bytes 4456448 | tf_op jit(solution)/shard_map/all_gather | solution.py:224
  81.5 37.8 %copy-start.4 = (bf16[512,1024]{1,0:T(8,128)(2,1)S(1)}, bf16[512,1024]{1,0:T(8,128)(2,1)}, u32[]{:S(2)}) copy-start(bf16[512,1024]{1,0:T(8,128)(2,1)} %param.12) | copy-start | bytes 3145732
  119.3 98.5 %copy-start.5 = (f32[1024]{0:T(1024)S(1)}, f32[1024]{0:T(1024)}, u32[]{:S(2)}) copy-start(f32[1024]{0:T(1024)} %param.16) | copy-start | bytes 12292
  122.6 1.3 copy-start.2
  237.9 224.4 %all-to-all-start = ((bf16[16,4,16,1024]{3,2,1,0:T(8,128)(2,1)}), bf16[16,4,16,1024]{3,2,1,0:T(8,128)(2,1)}, u32[]{:S(2)}, u32[]{:S(2)}) async-start(bf16[16,4,16,1024]{3,2,1,0:T(8,128)(2,1)} %bitcast.10), calls=%async_computation | async-start | bytes 4194304 | tf_op jit(solution)/shard_map/all_to_all | solution.py:239
  245.2 3.6 copy-start.3
  245.2 148.7 %all-reduce.2.cloned.1.call-start = ((), (), s32[]{:S(2)}) async-start(), calls=%async_computation.5 | async-start | bytes 8388608 | tf_op jit(solution)/shard_map/psum | solution.py:249
  393.9 2.2 copy-start
  464.1 1.4 copy-start.1
Sparse Core Ops, SparseCore 0:
  9.6 62.4 all-gather.4
  74.3 39.0 all-gather.6
  115.6 50.1 all-gather.10
  167.8 49.8 all-gather.8
  249.4 144.4 all-reduce.1
